TPU v7x, 256 devices: a whole 4x4x8 slice. The times are simulated.
256 devices in a mesh: group: 2 (over core), dp: 16 (over x, y), head: 8 (over z).
Axes of the slice: x: 4, y: 4, z: 8, core: 2. Of those that a mesh axis runs over, the one named last changes fastest.
Arguments:
- queries: bfloat16 [2, 512, 64, 576], P('group', 'dp', 'head'), may hold values from -400 to 400
- latent_cache: bfloat16 [2, 512, 192, 576], P('group', 'dp'), may hold values from -9 to 9
- lengths: int32 [2, 512], P('group', 'dp'), may hold values from 2 to 192, as said below
- w_value: bfloat16 [64, 512, 128], P('head'), may hold values from -0.25 to 0.25
- w_out: bfloat16 [8192, 7168], P('head', 'dp'), may hold values from -0.0625 to 0.0625
- residual: bfloat16 [2, 512, 7168], P('group', ('dp', 'head')), may hold values from -6 to 6
- norm_gain: float32 [7168], replicated, may hold values from 0.5 to 1.5
- routes: int32 [2, 512, 8], P('group', ('dp', 'head')), may hold values from 0 to 15, all different within a row; in each aligned block of 4 rows (0 to 3, 4 to 7, ..., all dimensions but the last counted through in order) at most 3 rows name the same one
- gate_weights: float32 [2, 512, 8], P('group', ('dp', 'head')), may hold values from 0.2 to 1
- w_gate: bfloat16 [16, 7168, 2048], P('dp', None, ('group', 'head')), may hold values from -0.0625 to 0.0625
- w_up: bfloat16 [16, 7168, 2048], P('dp', None, ('group', 'head')), may hold values from -0.0625 to 0.0625
- w_down: bfloat16 [16, 7168, 2048], P('dp', None, ('group', 'head')), may hold values from -0.125 to 0.125
Outputs:
- layer_out: bfloat16 [2, 512, 7168], P('group', ('dp', 'head'))
Inputs may be any that keep to these rules, and one draw needn't show every extreme that they name: `lengths`: some request has exactly 192 cached tokens. `routes`: the 8 experts of a token differ; among the 4 rows of one device (aligned blocks along the requests of both micro-batches in order) no expert is named by more than 3 rows, and that bound is reached.
All inputs are finite; a program needn't handle non-finite values.
Results may differ from a plain program's by a relative error of at most 0.029.
Values may be sent and summed in bfloat16 or wider, within the bound.
No kernel may reach another device: no remote copies, remote signals or barrier semaphores. Data moves between devices by JAX's collectives and lax.ppermute only.
A program may use at most 128 MiB of HBM per device.

v0:
```python
import jax
import jax.numpy as jnp
from jax import lax
from jax.sharding import PartitionSpec as P

EXPERTS = 16
CAP = 3


softmax_scale = 0.07216878364870323
norm_eps = 1e-06


def local(
    queries,
    latent_cache,
    lengths,
    w_value,
    w_out,
    residual,
    norm_gain,
    routes,
    gate_weights,
    w_gate,
    w_up,
    w_down,
):
    reqs_dev = queries.shape[1]
    heads_dev = queries.shape[2]
    latent_width = w_value.shape[1]
    value_width = w_value.shape[2]
    span = latent_cache.shape[2]
    model_width = residual.shape[2]
    local_experts = w_gate.shape[0]
    cached = latent_cache[0]
    scores = (
        jnp.einsum("rhc,rlc->rhl", queries[0], cached, preferred_element_type=jnp.float32)
        * softmax_scale
    )
    visible = lax.broadcasted_iota(jnp.int32, (reqs_dev, 1, span), 2) < lengths[0][:, None, None]
    scores = jnp.where(visible, scores, -jnp.inf)
    row_max = jnp.max(scores, axis=2, keepdims=True)
    weights = jnp.exp(scores - row_max)
    shares = (weights / jnp.sum(weights, axis=2, keepdims=True)).astype(jnp.bfloat16)
    latent = jnp.einsum(
        "rhl,rlc->rhc", shares, cached[:, :, :latent_width], preferred_element_type=jnp.float32
    ).astype(jnp.bfloat16)
    head_rows = jnp.einsum(
        "rhc,hcv->rhv", latent, w_value, preferred_element_type=jnp.float32
    ).astype(jnp.bfloat16)
    head_rows = head_rows.reshape(reqs_dev, heads_dev * value_width)
    partial_value = jnp.dot(
        lax.all_gather(head_rows, "dp", axis=0, tiled=True),
        w_out,
        preferred_element_type=jnp.float32,
    )
    summed = lax.psum_scatter(
        partial_value.astype(jnp.bfloat16), "head", scatter_dimension=1, tiled=True
    )
    attended = lax.all_to_all(summed, ("dp", "head"), split_axis=0, concat_axis=1, tiled=True)
    hidden = (residual[0].astype(jnp.float32) + attended.astype(jnp.float32)).astype(jnp.bfloat16)
    hidden_f = hidden.astype(jnp.float32)
    mean_square = jnp.mean(hidden_f * hidden_f, axis=1, keepdims=True)
    normed = (hidden_f * lax.rsqrt(mean_square + norm_eps) * norm_gain).astype(jnp.bfloat16)
    expert_ids = jnp.arange(EXPERTS, dtype=jnp.int32)
    chosen = (routes[0][:, :, None] == expert_ids[None, None, :]).astype(jnp.float32)
    member = jnp.sum(chosen, axis=1)
    weight_table = jnp.sum(gate_weights[0][:, :, None] * chosen, axis=1)
    before = jnp.cumsum(member, axis=0) - member
    slot_ids = jnp.arange(CAP, dtype=jnp.float32)
    placed = (
        member.T[:, None, :] * (before.T[:, None, :] == slot_ids[None, :, None]).astype(jnp.float32)
    ).astype(jnp.bfloat16)
    packed = jnp.einsum("eck,kd->ecd", placed, normed, preferred_element_type=jnp.float32).astype(
        jnp.bfloat16
    )
    arrived = lax.all_to_all(packed, "dp", split_axis=0, concat_axis=0, tiled=True)
    slot_rows = arrived.reshape(-1, local_experts, CAP, model_width)
    block_rows = lax.all_gather(slot_rows, ("group", "head"), axis=0, tiled=True)
    gate = jnp.einsum("slcd,ldf->slcf", block_rows, w_gate, preferred_element_type=jnp.float32)
    upward = jnp.einsum("slcd,ldf->slcf", block_rows, w_up, preferred_element_type=jnp.float32)
    activated = (jax.nn.silu(gate) * upward).astype(jnp.bfloat16)
    expert_sums = lax.psum_scatter(
        jnp.einsum("slcf,ldf->slcd", activated, w_down, preferred_element_type=jnp.float32).astype(
            jnp.bfloat16
        ),
        ("group", "head"),
        scatter_dimension=0,
        tiled=True,
    )
    results = expert_sums.reshape(-1, CAP, model_width)
    returned = lax.all_to_all(results, "dp", split_axis=0, concat_axis=0, tiled=True)
    gathered_rows = jnp.einsum("eck,ecd->ked", placed, returned, preferred_element_type=jnp.float32)
    mixture = jnp.einsum("ke,ked->kd", weight_table, gathered_rows)
    layer_out = (hidden_f + mixture).astype(jnp.bfloat16)
    return layer_out[None]


def solution(mesh):
    in_specs = (
        P("group", "dp", "head", None),
        P("group", "dp", None, None),
        P("group", "dp"),
        P("head", None, None),
        P("head", "dp"),
        P("group", ("dp", "head"), None),
        P(),
        P("group", ("dp", "head"), None),
        P("group", ("dp", "head"), None),
        P("dp", None, ("group", "head")),
        P("dp", None, ("group", "head")),
        P("dp", None, ("group", "head")),
    )
    out_specs = P("group", ("dp", "head"), None)
    return jax.shard_map(local, mesh=mesh, in_specs=in_specs, out_specs=out_specs, check_vma=False)
```

profile of v0, /device:TPU:8, one launch (start us, length us, event | category | flops | bytes accessed | tf_op | source)
XLA Modules:
  0.0 393.6 jit_solution(12691266057905356293)
XLA Ops:
  6.5 0.0 copy-start
  6.5 0.0 copy-start.1
  6.5 0.0 all-gather.4.cloned.1.call-start
  6.5 0.9 iota_compare_fusion.1
  7.4 6.1 %fusion.57 = (f32[32,8]{1,0:T(8,128)S(1)}, f32[32,8,192]{2,1,0:T(8,128)S(1)}) fusion(bf16[1,32,8,576]{3,2,1,0:T(8,128)(2,1)} %param.12, pred[32,192]{1,0:T(8,128)(4,1)S(1)} %iota_compare_fusion.1, bf16[1,32,192,576]{3,2,1,0:T(8,128)(2,1)} %param.13), kind=kOutput, calls=%fused_computation.62 | convolution fusion | flops 56819904 | bytes 7576576 | tf_op jit(solution)/shard_map/sub | solution.py:43
  13.5 0.0 copy-start.4
  13.5 0.0 copy-start.5
  13.5 0.0 copy-start.2
  13.5 0.0 copy-start.3
  13.5 3.8 fusion.18
  17.3 0.0 copy-done.1
  17.3 0.3 fusion.32
  17.7 0.6 copy.47
  18.3 0.0 all-gather.4.cloned.1.call-update
  18.3 0.0 reduce-scatter.3.cloned.1.call-start
  18.4 50.2 %all-gather.4.cloned.1.call-done = bf16[512,1024]{1,0:T(8,128)(2,1)} async-done(((bf16[32,1024]{1,0:T(8,128)(2,1)}), bf16[512,1024]{1,0:T(8,128)(2,1)}) %all-gather.4.cloned.1.call-update) | async-done | bytes 1048592 | tf_op jit(solution)/shard_map/all_gather | solution.py:53
  68.6 2.9 convolution_convert_fusion.2
  71.6 0.0 reduce-scatter.3.cloned.1.call-update
  71.6 0.0 copy-done.4
  71.6 0.0 copy-done.5
  71.6 0.1 convert_reduce_fusion
  71.7 0.1 copy.30
  71.8 0.1 copy.29
  71.9 36.8 %reduce-scatter.3.cloned.1.call-done = bf16[512,56]{0,1:T(8,128)(2,1)} async-done(((bf16[512,448]{0,1:T(8,128)(2,1)}), bf16[512,56]{0,1:T(8,128)(2,1)}) %reduce-scatter.3.cloned.1.call-update) | async-done | bytes 57360 | tf_op jit(solution)/shard_map/reduce_scatter | solution.py:57
  108.7 1.6 copy.27
  110.2 11.1 %all-to-all-start = ((bf16[128,4,56]{2,1,0:T(4,128)(2,1)}), bf16[128,4,56]{2,1,0:T(4,128)(2,1)S(1)}, u32[]{:S(2)}, u32[]{:S(2)}) async-start(bf16[128,4,56]{2,1,0:T(4,128)(2,1)} %bitcast.5), calls=%async_computation.1 | async-start | bytes 262144 | tf_op jit(solution)/shard_map/all_to_all | solution.py:60
  121.3 0.0 all-gather.6.cloned.1.call-start
  121.4 0.1 select_convert_fusion
  121.5 0.1 copy.31
  121.6 11.1 %all-to-all-done = bf16[128,4,56]{2,1,0:T(4,128)(2,1)S(1)} async-done(((bf16[128,4,56]{2,1,0:T(4,128)(2,1)}), bf16[128,4,56]{2,1,0:T(4,128)(2,1)S(1)}, u32[]{:S(2)}, u32[]{:S(2)}) %all-to-all-start) | async-done | bytes 57376 | tf_op jit(solution)/shard_map/all_to_all | solution.py:60
  132.8 0.2 reshape.81
  133.0 0.0 copy-done.2
  133.0 0.2 fusion.44
  133.2 0.0 copy-done.3
  133.2 0.4 convolution_convert_fusion.1
  133.6 0.6 copy.32
  134.2 14.7 %all_to_all.23 = bf16[16,3,7168]{2,1,0:T(4,128)(2,1)S(1)} all-to-all(bf16[16,3,7168]{2,1,0:T(4,128)(2,1)S(1)} %copy.32), channel_id=1, replica_groups=mesh['group'=2,'dp'=16,'head'=8] {'dp'}, dimensions={0} | all-to-all | bytes 1376256 | tf_op jit(solution)/shard_map/all_to_all | solution.py:77
  148.9 1.1 copy.33
  150.1 0.0 all-gather.6.cloned.1.call-update
  150.1 0.2 reduce-scatter.5.cloned.1.call-start
  150.3 63.1 %all-gather.6.cloned.1.call-done = bf16[256,3,7168]{2,0,1:T(8,128)(2,1)} async-done(((bf16[16,3,7168]{2,0,1:T(8,128)(2,1)}), bf16[256,3,7168]{2,0,1:T(8,128)(2,1)}) %all-gather.6.cloned.1.call-update) | async-done | bytes 11010064 | tf_op jit(solution)/shard_map/all_gather | solution.py:79
  213.5 6.3 %fusion.12 = f32[256,1,3,128]{3,0,2,1:T(8,128)S(1)} fusion(bf16[256,3,7168]{2,0,1:T(8,128)(2,1)} %all-gather.6.cloned.1.call-done, bf16[1,7168,128]{2,1,0:T(8,128)(2,1)} %param.21), kind=kOutput, calls=%fused_computation.16 | convolution fusion | flops 1409286144 | bytes 13238272 | tf_op jit(solution)/shard_map/slcd,ldf->slcf/dot_general | solution.py:80
  219.8 0.0 copy-done
  219.8 17.3 %fusion.1 = bf16[256,1,3,7168]{3,0,2,1:T(8,128)(2,1)} fusion(bf16[1,7168,128]{2,1,0:T(8,128)(2,1)S(1)} %copy-done, bf16[256,3,7168]{2,0,1:T(8,128)(2,1)} %all-gather.6.cloned.1.call-done, bf16[1,7168,128]{2,1,0:T(8,128)(2,1)} %param.22, f32[256,1,3,128]{3,0,2,1:T(8,128)S(1)} %fusion.12), kind=kOutput, calls=%fused_computation.2 | convolution fusion | flops 2824667136 | bytes 26083328 | tf_op jit(solution)/shard_map/slcf,ldf->slcd/dot_general | solution.py:84
  237.1 0.0 reduce-scatter.5.cloned.1.call-update
  237.1 125.1 %reduce-scatter.5.cloned.1.call-done = bf16[16,1,3,7168]{3,0,2,1:T(8,128)(2,1)} async-done(((bf16[256,1,3,7168]{3,0,2,1:T(8,128)(2,1)}), bf16[16,1,3,7168]{3,0,2,1:T(8,128)(2,1)}) %reduce-scatter.5.cloned.1.call-update) | async-done | bytes 688144 | tf_op jit(solution)/shard_map/reduce_scatter | solution.py:83
  362.3 1.7 copy.34
  364.0 21.1 %all_to_all.24 = bf16[16,3,7168]{2,1,0:T(4,128)(2,1)S(1)} all-to-all(bf16[16,3,7168]{2,1,0:T(4,128)(2,1)S(1)} %copy.34), channel_id=1, replica_groups=mesh['group'=2,'dp'=16,'head'=8] {'dp'}, dimensions={0} | all-to-all | bytes 1376256 | tf_op jit(solution)/shard_map/all_to_all | solution.py:92
  385.1 0.7 convolution_bitcast_fusion
  385.8 0.6 fusion.9
  386.4 0.7 fusion.49
  (5 shorter events, 0.1 us)
Async XLA Ops:
  6.5 213.3 %copy-start = (bf16[1,7168,128]{2,1,0:T(8,128)(2,1)S(1)}, bf16[1,7168,128]{2,1,0:T(8,128)(2,1)}, u32[]{:S(2)}) copy-start(bf16[1,7168,128]{2,1,0:T(8,128)(2,1)} %param.23) | copy-start | bytes 5505028
  6.5 10.8 %copy-start.1 = (bf16[8,512,128]{2,1,0:T(8,128)(2,1)S(1)}, bf16[8,512,128]{2,1,0:T(8,128)(2,1)}, u32[]{:S(2)}) copy-start(bf16[8,512,128]{2,1,0:T(8,128)(2,1)} %param.15) | copy-start | bytes 3145732
  6.5 62.1 %all-gather.4.cloned.1.call-start = ((), (), s32[]{:S(2)}) async-start(), calls=%async_computation.5 | async-start | bytes 1114112 | tf_op jit(solution)/shard_map/all_gather | solution.py:53
  13.5 58.1 %copy-start.4 = (s32[1,4,8]{2,1,0:T(4,128)S(1)}, s32[1,4,8]{2,1,0:T(4,128)}, u32[]{:S(2)}) copy-start(s32[1,4,8]{2,1,0:T(4,128)} %param.19) | copy-start | bytes 388
  13.5 58.1 %copy-start.5 = (f32[1,4,8]{2,1,0:T(4,128)S(1)}, f32[1,4,8]{2,1,0:T(4,128)}, u32[]{:S(2)}) copy-start(f32[1,4,8]{2,1,0:T(4,128)} %param.20) | copy-start | bytes 388
  13.5 119.5 %copy-start.2 = (bf16[1,4,7168]{2,1,0:T(4,128)(2,1)S(1)}, bf16[1,4,7168]{2,1,0:T(4,128)(2,1)}, u32[]{:S(2)}) copy-start(bf16[1,4,7168]{2,1,0:T(4,128)(2,1)} %param.17) | copy-start | bytes 172036
  13.5 119.7 %copy-start.3 = (f32[7168]{0:T(1024)S(1)}, f32[7168]{0:T(1024)}, u32[]{:S(2)}) copy-start(f32[7168]{0:T(1024)} %param.18) | copy-start | bytes 86020
  18.3 90.4 %reduce-scatter.3.cloned.1.call-start = ((), (), s32[]{:S(2)}) async-start(), calls=%async_computation.6 | async-start | bytes 516096 | tf_op jit(solution)/shard_map/reduce_scatter | solution.py:57
  110.2 22.4 %all-to-all-start = ((bf16[128,4,56]{2,1,0:T(4,128)(2,1)}), bf16[128,4,56]{2,1,0:T(4,128)(2,1)S(1)}, u32[]{:S(2)}, u32[]{:S(2)}) async-start(bf16[128,4,56]{2,1,0:T(4,128)(2,1)} %bitcast.5), calls=%async_computation.1 | async-start | bytes 262144 | tf_op jit(solution)/shard_map/all_to_all | solution.py:60
  121.3 92.1 %all-gather.6.cloned.1.call-start = ((), (), s32[]{:S(2)}) async-start(), calls=%async_computation.8 | async-start | bytes 11698176 | tf_op jit(solution)/shard_map/all_gather | solution.py:79
  150.1 212.2 %reduce-scatter.5.cloned.1.call-start = ((), (), s32[]{:S(2)}) async-start(), calls=%async_computation.7 | async-start | bytes 11698176 | tf_op jit(solution)/shard_map/reduce_scatter | solution.py:83
Sparse Core Ops, SparseCore 0:
  18.4 50.1 all-gather.3
  71.7 36.9 reduce-scatter.2
  150.2 63.2 all-gather.5
  237.3 124.9 reduce-scatter.4
where the time goes:
time: 394 us
  waiting for transfers between devices  286 us (73%)
  matrix products  38.5 us (10%)
  blocking collectives  35.9 us (9%)
  between operations  13.3 us (3%)
  starting transfers between devices  11.4 us (3%)
  local copies, waits for them, and re-layouts  6.16 us (2%)
    reduce_scatter x1, waiting for transfers between devices, local(): lax.psum_scatter(jnp.einsum('slcf,ldf->slcd', activated, w_down, preferre...  125 us
    all_gather x1, waiting for transfers between devices, local(): lax.all_gather(slot_rows, ('group', 'head'), axis=0, tiled=True)  63.1 us
    all_gather x1, waiting for transfers between devices, local(): lax.all_gather(head_rows, 'dp', axis=0, tiled=True)  50.2 us
    reduce_scatter x1, waiting for transfers between devices, local(): lax.psum_scatter(partial_value.astype(jnp.bfloat16), 'head', scatter_dime...  36.8 us
    all_to_all x1, blocking collectives, local(): lax.all_to_all(results, 'dp', split_axis=0, concat_axis=0, tiled=True)  21.1 us
    dot_general x1, matrix products, local(): jnp.einsum('slcf,ldf->slcd', activated, w_down, preferred_element_type=jn...  17.3 us
    all_to_all x1, blocking collectives, local(): lax.all_to_all(packed, 'dp', split_axis=0, concat_axis=0, tiled=True)  14.7 us
    all_to_all x1, waiting for transfers between devices, local(): lax.all_to_all(summed, ('dp', 'head'), split_axis=0, concat_axis=1, tiled...  11.1 us
  transfers between devices with their start and end apart: 5, of which 5 were waited for; matrix products, arithmetic and copies ran while one was open for 0% of the time, Pallas kernels for 0%

commit v1 on v0

v1 whole, which is shorter than its diff:
```python
import jax
import jax.numpy as jnp
from jax import lax
from jax.sharding import PartitionSpec as P

EXPERTS = 16
CAP = 3


softmax_scale = 0.07216878364870323
norm_eps = 1e-06
bf16 = jnp.bfloat16
f32 = jnp.float32


def local(
    queries,
    latent_cache,
    lengths,
    w_value,
    w_out,
    residual,
    norm_gain,
    routes,
    gate_weights,
    w_gate,
    w_up,
    w_down,
):
    reqs = queries.shape[1]
    heads = queries.shape[2]
    latent_width = w_value.shape[1]
    value_width = w_value.shape[2]
    span = latent_cache.shape[2]
    rows = residual.shape[1]
    width = residual.shape[2]
    n_group = lax.axis_size("group")
    n_dp = lax.axis_size("dp")
    n_head = lax.axis_size("head")
    n_col = n_group * n_head
    cols = width // n_dp
    piece = width // n_col
    g = lax.axis_index("group")
    dp = lax.axis_index("dp")
    z = lax.axis_index("head")

    down = lax.all_to_all(
        w_down[0].reshape(n_col, piece, w_down.shape[2]),
        ("group", "head"),
        split_axis=0,
        concat_axis=0,
        tiled=True,
    )

    expert_ids = jnp.arange(EXPERTS, dtype=jnp.int32)
    chosen = routes[0][:, :, None] == expert_ids[None, None, :]
    table = jnp.max(jnp.where(chosen, gate_weights[0][:, :, None], -1.0), axis=1)
    table = lax.all_gather(table, ("group", "dp", "head"), axis=0, tiled=False)
    table = table.reshape(n_group, n_dp, n_head, rows, EXPERTS)

    cached = latent_cache[0]
    scores = (
        jnp.einsum("rhc,rlc->rhl", queries[0], cached, preferred_element_type=f32) * softmax_scale
    )
    visible = lax.broadcasted_iota(jnp.int32, (reqs, 1, span), 2) < lengths[0][:, None, None]
    scores = jnp.where(visible, scores, -jnp.inf)
    row_max = jnp.max(scores, axis=2, keepdims=True)
    weights = jnp.exp(scores - row_max)
    shares = (weights / jnp.sum(weights, axis=2, keepdims=True)).astype(bf16)
    latent = jnp.einsum(
        "rhl,rlc->rhc", shares, cached[:, :, :latent_width], preferred_element_type=f32
    ).astype(bf16)
    head_rows = jnp.einsum("rhc,hcv->hrv", latent, w_value, preferred_element_type=f32).astype(bf16)

    res = residual[0].reshape(rows, n_dp, cols).transpose(1, 0, 2).reshape(n_dp, -1, value_width)
    res_rows = res.shape[1]
    pad = -res_rows % 16
    send = jnp.concatenate(
        [
            jnp.broadcast_to(
                head_rows.reshape(1, heads * reqs, value_width),
                (n_dp, heads * reqs, value_width),
            ),
            jnp.pad(res, ((0, 0), (0, pad), (0, 0))),
        ],
        axis=1,
    )
    got = lax.all_to_all(send, "dp", split_axis=0, concat_axis=0, tiled=True)
    res_piece = got[:, heads * reqs : heads * reqs + res_rows].reshape(n_dp * rows, cols)
    values = got[:, : heads * reqs].reshape(n_dp, heads, n_head, rows, value_width)
    partial = jnp.einsum(
        "dhziv,hvc->zdic",
        values,
        w_out.reshape(heads, value_width, cols),
        preferred_element_type=f32,
    ).astype(bf16)
    partial = lax.all_to_all(
        partial.reshape(n_head, n_dp * rows, cols), "head", split_axis=0, concat_axis=0, tiled=True
    )
    attended = jnp.sum(partial.astype(f32), axis=0).astype(bf16)
    hidden_piece = (res_piece.astype(f32) + attended.astype(f32)).astype(bf16)

    hidden = lax.all_to_all(
        jnp.broadcast_to(hidden_piece[None], (n_dp,) + hidden_piece.shape),
        "dp",
        split_axis=0,
        concat_axis=0,
        tiled=True,
    )
    hidden = hidden.transpose(1, 0, 2).reshape(n_dp * rows, width)
    hidden_f = hidden.astype(f32)
    mean_square = jnp.mean(hidden_f * hidden_f, axis=1, keepdims=True)
    normed = (hidden_f * lax.rsqrt(mean_square + norm_eps) * norm_gain).astype(bf16)
    home = lax.dynamic_slice(hidden, (dp * rows, 0), (rows, width))

    slot_ids = jnp.arange(CAP, dtype=jnp.int32)
    mine = lax.dynamic_index_in_dim(lax.dynamic_index_in_dim(table, g, 0, False), z, 1, False)
    mine = lax.dynamic_index_in_dim(mine, dp, 2, False) > 0
    before = jnp.cumsum(mine.astype(jnp.int32), axis=1) - mine
    placed = mine[:, None, :] & (before[:, None, :] == slot_ids[None, :, None])
    same = jnp.eye(n_dp, dtype=bool)
    pack = (placed[:, :, None, :] & same[:, None, :, None]).reshape(n_dp * CAP, n_dp * rows)
    packed = jnp.dot(pack.astype(bf16), normed, preferred_element_type=f32).astype(bf16)
    block = lax.all_gather(packed, ("group", "head"), axis=0, tiled=True)

    gate = jnp.dot(block, w_gate[0], preferred_element_type=f32)
    upward = jnp.dot(block, w_up[0], preferred_element_type=f32)
    active = (jax.nn.silu(gate) * upward).astype(bf16)
    active = (
        active.reshape(n_col, n_dp, CAP, -1).transpose(1, 0, 2, 3).reshape(n_col * n_dp * CAP, -1)
    )
    actives = lax.all_gather(active, ("group", "head"), axis=0, tiled=False)
    out = jnp.einsum("srf,scf->rc", actives, down, preferred_element_type=f32).astype(bf16)
    back = lax.all_to_all(
        out.reshape(n_dp, n_col * CAP, piece), "dp", split_axis=0, concat_axis=0, tiled=True
    )

    ours = lax.dynamic_index_in_dim(table, dp, 1, False).reshape(n_col, rows, EXPERTS)
    taken = ours > 0
    ahead = jnp.cumsum(taken.astype(jnp.int32), axis=1) - taken
    spread = jnp.where(
        taken[..., None] & (ahead[..., None] == slot_ids), ours[..., None], 0.0
    )
    mix = jnp.where(
        jnp.eye(n_col, dtype=bool)[:, None, None, :, None], spread[:, :, :, None, :], 0.0
    ).reshape(n_col * rows, EXPERTS * n_col * CAP)
    mix_high = mix.astype(bf16)
    mix_low = (mix - mix_high.astype(f32)).astype(bf16)
    back = back.reshape(EXPERTS * n_col * CAP, piece)
    mixed = jnp.dot(mix_high, back, preferred_element_type=f32) + jnp.dot(
        mix_low, back, preferred_element_type=f32
    )
    mixed = lax.all_to_all(
        mixed.astype(bf16).reshape(n_col, rows, piece),
        ("group", "head"),
        split_axis=0,
        concat_axis=0,
        tiled=True,
    )
    mixture = mixed.transpose(1, 0, 2).reshape(rows, width)
    layer_out = (home.astype(f32) + mixture.astype(f32)).astype(bf16)
    return layer_out[None]


def solution(mesh):
    in_specs = (
        P("group", "dp", "head", None),
        P("group", "dp", None, None),
        P("group", "dp"),
        P("head", None, None),
        P("head", "dp"),
        P("group", ("dp", "head"), None),
        P(),
        P("group", ("dp", "head"), None),
        P("group", ("dp", "head"), None),
        P("dp", None, ("group", "head")),
        P("dp", None, ("group", "head")),
        P("dp", None, ("group", "head")),
    )
    out_specs = P("group", ("dp", "head"), None)
    return jax.shard_map(local, mesh=mesh, in_specs=in_specs, out_specs=out_specs, check_vma=False)
```

time: 394 us -> 907 us (2.30)
  blocking collectives: 35.9 us -> 606 us
  waiting for transfers between devices: 286 us -> 172 us
  starting transfers between devices: 11.4 us -> 38.5 us
  local copies, waits for them, and re-layouts: 6.16 us -> 32 us
  other arithmetic: 1.99 us -> 12.4 us
    all_gather x0 -> x1, blocking collectives: none -> 606 us  [local(): table = lax.all_gather(table, ('group', 'dp', 'head'), axis=0, tiled=False)]
    reduce_scatter x2 -> x0, waiting for transfers between devices: 162 us -> none  [the longest x1 125 us: local(): lax.psum_scatter(jnp.einsum('slcf,ldf->slcd', activated, w_down, preferre...]
    all_to_all x1 -> x6, waiting for transfers between devices: 11.1 us -> 88.1 us  [the longest x1 53.9 us: local(): lax.all_to_all(w_down[0].reshape(n_col, piece, w_down.shape[2]), ('group'...]
    all_to_all x2 -> x0, blocking collectives: 35.9 us -> none  [the longest x1 21.1 us: local(): lax.all_to_all(results, 'dp', split_axis=0, concat_axis=0, tiled=True)]
    all_gather x2, waiting for transfers between devices: 113 us -> 83.6 us  [the longest x1 78.1 us: local(): block = lax.all_gather(packed, ('group', 'head'), axis=0, tiled=True)]
    all_to_all x1 -> x6, starting transfers between devices: 11.1 us -> 38.3 us  [the longest x1 8.47 us: local(): lax.all_to_all(partial.reshape(n_head, n_dp * rows, cols), 'head', split_...]
    convert_element_type x4 -> x8, local copies, waits for them, and re-layouts: 0.94 us -> 16.4 us  [the longest x1 4.71 us: local(): mix_high = mix.astype(bf16)]
    dot_general x7 -> x8, matrix products: 28.6 us -> 21.1 us  [the longest x1 6.88 us: local(): gate = jnp.dot(block, w_gate[0], preferred_element_type=f32)]
  transfers between devices with their start and end apart: 5 -> 8, of which waited for: 5 -> 6; matrix products, arithmetic and copies ran while one was open for 0% -> 3% of each run, Pallas kernels for 0% -> 0%
where the time goes in v1:
time: 907 us; the launch traced here: 905 us
  blocking collectives  606 us (67%)
  waiting for transfers between devices  172 us (19%)
  starting transfers between devices  38.5 us (4%)
  local copies, waits for them, and re-layouts  32 us (4%)
  matrix products  31 us (3%)
  between operations  13.7 us (2%)
  other arithmetic  12.4 us (1%)
    all_gather x1, blocking collectives, local(): table = lax.all_gather(table, ('group', 'dp', 'head'), axis=0, tiled=False)  606 us
    all_gather x1, waiting for transfers between devices, local(): block = lax.all_gather(packed, ('group', 'head'), axis=0, tiled=True)  78.1 us
    all_to_all x1, waiting for transfers between devices, local(): lax.all_to_all(w_down[0].reshape(n_col, piece, w_down.shape[2]), ('group'...  53.9 us
  transfers between devices with their start and end apart: 8, of which 6 were waited for; matrix products, arithmetic and copies ran while one was open for 3% of the time, Pallas kernels for 0%

profile of v1, /device:TPU:8, one launch (start us, length us, event | category | flops | bytes accessed | tf_op | source)
XLA Modules:
  0.0 905.1 jit_solution(1191984066099399660)
XLA Ops:
  6.5 0.9 iota_compare_fusion.3
  7.4 0.9 reshape_squeeze.6
  8.4 0.1 reshape.206
  8.5 6.1 fusion.39
  14.6 3.8 fusion.15
  18.4 0.3 convolution_convert_fusion.1
  18.8 0.2 broadcast_in_dim.92
  19.0 1.1 fusion.27
  20.1 7.5 all-to-all-start
  27.6 1.2 copy.123
  28.8 16.1 %all-to-all-done = bf16[16,272,128]{2,1,0:T(8,128)(2,1)} async-done(((bf16[16,272,128]{2,1,0:T(8,128)(2,1)}), bf16[16,272,128]{2,1,0:T(8,128)(2,1)}, u32[]{:S(2)}, u32[]{:S(2)}) %all-to-all-start) | async-done | bytes 1114144 | tf_op jit(solution)/shard_map/all_to_all | solution.py:88
  44.9 1.4 slice.14
  46.3 0.7 copy.122
  47.0 0.8 fusion.13
  47.8 1.0 copy.105
  48.7 8.5 all-to-all-start.1
  57.2 0.9 slice_convert_fusion
  58.1 0.1 reshape.217
  58.2 13.9 %all-to-all-done.1 = bf16[8,64,448]{2,1,0:T(8,128)(2,1)S(1)} async-done(((bf16[8,64,448]{2,1,0:T(8,128)(2,1)}), bf16[8,64,448]{2,1,0:T(8,128)(2,1)S(1)}, u32[]{:S(2)}, u32[]{:S(2)}) %all-to-all-start.1) | async-done | bytes 458784 | tf_op jit(solution)/shard_map/all_to_all | solution.py:97
  72.2 1.1 broadcast_in_dim.93
  73.3 5.7 all-to-all-start.2
  79.1 605.8 %all-gather.1 = f32[256,4,16]{2,1,0:T(4,128)S(1)} all-gather(f32[1,4,16]{2,1,0:T(4,128)S(1)} %bitcast.96), channel_id=2, replica_groups=mesh['group'=2,'dp'=16,'head'=8] {'group','dp','head'}, dimensions={0}, use_global_device_ids=true | all-gather | bytes 65792 | tf_op jit(solution)/shard_map/all_gather | solution.py:58
  685.0 1.3 compare_reduce_fusion
  686.3 0.1 copy.111
  686.7 0.1 broadcast_and_fusion
  686.8 0.2 and.57
  687.0 0.8 mul.46
  687.9 0.3 fusion.5
  688.2 0.3 fusion.7
  688.5 1.6 copy.114
  690.1 2.9 convert_element_type.163
  693.0 2.4 convolution_convert_fusion
  695.4 0.2 all-gather.7.cloned.1.call-start
  695.6 78.1 %all-gather.5.cloned.1.call-done = bf16[768,7168]{1,0:T(8,128)(2,1)} async-done(((bf16[48,7168]{1,0:T(8,128)(2,1)}), bf16[768,7168]{1,0:T(8,128)(2,1)}) %all-gather.5.cloned.1.call-update) | async-done | bytes 11010064 | tf_op jit(solution)/shard_map/all_gather | solution.py:124
  773.7 6.9 fusion.10
  780.6 0.4 copy-done.7
  781.0 0.5 copy-done.8
  781.5 3.0 fusion.23
  784.6 0.1 copy.115
  784.8 0.8 all_gather_reshape.3
  785.6 4.4 all-to-all-start.3
  790.1 0.8 broadcast_compare_fusion
  790.8 0.8 copy.108
  791.6 0.2 copy.109
  791.8 0.2 copy.110
  792.0 53.9 %all-to-all-done.3 = bf16[16,448,128]{2,1,0:T(8,128)(2,1)} async-done(((bf16[16,448,128]{2,1,0:T(8,128)(2,1)}), bf16[16,448,128]{2,1,0:T(8,128)(2,1)}, u32[]{:S(2)}, u32[]{:S(2)}) %all-to-all-start.3) | async-done | bytes 1835040 | tf_op jit(solution)/shard_map/all_to_all | solution.py:47
  845.9 5.6 all-gather.7.cloned.1.call-done
  851.5 4.9 fusion.12
  856.4 2.2 copy.116
  858.6 7.3 all-to-all-start.4
  865.9 0.8 fusion.31
  866.7 2.4 select_convert_fusion
  869.1 4.7 convert_element_type.159
  873.8 2.5 fusion.1
  876.3 4.7 convert_element_type.169
  881.1 1.4 fusion.44
  882.5 1.4 fusion.26
  883.9 0.6 reshape.216
  884.5 4.9 all-to-all-start.5
  889.4 1.6 copy.106
  890.9 2.2 reshape.210
  893.1 4.2 all-to-all-done.5
  897.4 0.1 reshape.218
  897.5 0.7 fusion.35
  (38 shorter events, 0.8 us)
Async XLA Ops:
  6.5 767.2 %copy-start = (bf16[1,7168,128]{2,1,0:T(8,128)(2,1)S(1)}, bf16[1,7168,128]{2,1,0:T(8,128)(2,1)}, u32[]{:S(2)}) copy-start(bf16[1,7168,128]{2,1,0:T(8,128)(2,1)} %param.21) | copy-start | bytes 5505028
  14.6 3.8 copy-start.1
  20.1 7.5 copy-start.2
  20.1 24.8 %all-to-all-start = ((bf16[16,272,128]{2,1,0:T(8,128)(2,1)}), bf16[16,272,128]{2,1,0:T(8,128)(2,1)}, u32[]{:S(2)}, u32[]{:S(2)}) async-start(bf16[16,272,128]{2,1,0:T(8,128)(2,1)} %fusion.27), calls=%async_computation | async-start | bytes 2228224 | tf_op jit(solution)/shard_map/all_to_all | solution.py:88
  44.9 2.1 copy-start.3
  48.7 23.3 %all-to-all-start.1 = ((bf16[8,64,448]{2,1,0:T(8,128)(2,1)}), bf16[8,64,448]{2,1,0:T(8,128)(2,1)S(1)}, u32[]{:S(2)}, u32[]{:S(2)}) async-start(bf16[8,64,448]{2,1,0:T(8,128)(2,1)} %copy.105), calls=%async_computation.1 | async-start | bytes 1048576 | tf_op jit(solution)/shard_map/all_to_all | solution.py:97
  57.2 21.8 %copy-start.5 = (f32[1,4,8]{2,1,0:T(4,128)S(1)}, f32[1,4,8]{2,1,0:T(4,128)}, u32[]{:S(2)}) copy-start(f32[1,4,8]{2,1,0:T(4,128)} %param.20) | copy-start | bytes 388
  57.2 21.8 %copy-start.6 = (s32[1,4,8]{2,1,0:T(4,128)S(1)}, s32[1,4,8]{2,1,0:T(4,128)}, u32[]{:S(2)}) copy-start(s32[1,4,8]{2,1,0:T(4,128)} %param.19) | copy-start | bytes 388
  73.3 614.6 %all-to-all-start.2 = ((bf16[16,64,448]{2,1,0:T(8,128)(2,1)}), bf16[16,64,448]{2,1,0:T(8,128)(2,1)S(1)}, u32[]{:S(2)}, u32[]{:S(2)}) async-start(bf16[16,64,448]{2,1,0:T(8,128)(2,1)} %broadcast_in_dim.93), calls=%async_computation.2 | async-start | bytes 2097152 | tf_op jit(solution)/shard_map/all_to_all | solution.py:103
  79.0 694.7 %all-gather.5.cloned.1.call-start = ((), (), s32[]{:S(2)}) async-start(), calls=%async_computation.6 | async-start | bytes 11698176 | tf_op jit(solution)/shard_map/all_gather | solution.py:124
  685.0 5.1 copy-start.4
  695.4 156.1 %all-gather.7.cloned.1.call-start = ((), (), s32[]{:S(2)}) async-start(), calls=%async_computation.7 | async-start | bytes 3342336 | tf_op jit(solution)/shard_map/all_gather | solution.py:132
  773.7 7.3 copy-start.7
  773.7 7.8 copy-start.8
  785.6 60.3 %all-to-all-start.3 = ((bf16[16,448,128]{2,1,0:T(8,128)(2,1)}), bf16[16,448,128]{2,1,0:T(8,128)(2,1)}, u32[]{:S(2)}, u32[]{:S(2)}) async-start(bf16[16,448,128]{2,1,0:T(8,128)(2,1)} %bitcast.86), calls=%async_computation.3 | async-start | bytes 3670016 | tf_op jit(solution)/shard_map/all_to_all | solution.py:47
  858.6 22.4 %all-to-all-start.4 = ((bf16[16,48,448]{2,1,0:T(8,128)(2,1)}), bf16[16,48,448]{2,1,0:T(8,128)(2,1)}, u32[]{:S(2)}, u32[]{:S(2)}) async-start(bf16[16,48,448]{2,1,0:T(8,128)(2,1)} %bitcast.85), calls=%async_computation.4 | async-start | bytes 1572864 | tf_op jit(solution)/shard_map/all_to_all | solution.py:134
  884.5 12.8 %all-to-all-start.5 = ((bf16[16,4,448]{2,1,0:T(4,128)(2,1)}), bf16[16,4,448]{2,1,0:T(4,128)(2,1)S(1)}, u32[]{:S(2)}, u32[]{:S(2)}) async-start(bf16[16,4,448]{2,1,0:T(4,128)(2,1)} %reshape.216), calls=%async_computation.5 | async-start | bytes 131072 | tf_op jit(solution)/shard_map/all_to_all | solution.py:153
Sparse Core Ops, SparseCore 0:
  695.5 78.1 all-gather.4
  785.7 65.6 all-gather.6

commit v2 on v1

--- a/solution.py
+++ b/solution.py
@@ -44,19 +44,29 @@
     dp = lax.axis_index("dp")
     z = lax.axis_index("head")
 
-    down = lax.all_to_all(
-        w_down[0].reshape(n_col, piece, w_down.shape[2]),
+    slabs = w_down[0].reshape(n_group, n_head, piece, w_down.shape[2])
+
+    def shifted(k):
+        slab = lax.dynamic_index_in_dim(slabs, lax.rem(z + k, n_head), 1, False)
+        if k == 0:
+            return slab
+        return lax.ppermute(slab, "head", [(i, (i + k) % n_head) for i in range(n_head)])
+
+    shifts = [shifted(k) for k in range(n_head)]
+
+    expert_ids = jnp.arange(EXPERTS, dtype=jnp.int32)
+    chosen = routes[0][:, :, None] == expert_ids[None, None, :]
+    table = jnp.max(jnp.where(chosen, gate_weights[0][:, :, None], -1.0), axis=1)
+    table_high = table.astype(bf16)
+    table_low = (table - table_high.astype(f32)).astype(bf16)
+    info = jnp.concatenate([table_high, table_low], axis=1)
+    info = lax.all_to_all(
+        jnp.broadcast_to(info[None], (n_col,) + info.shape),
         ("group", "head"),
         split_axis=0,
         concat_axis=0,
         tiled=True,
-    )
-
-    expert_ids = jnp.arange(EXPERTS, dtype=jnp.int32)
-    chosen = routes[0][:, :, None] == expert_ids[None, None, :]
-    table = jnp.max(jnp.where(chosen, gate_weights[0][:, :, None], -1.0), axis=1)
-    table = lax.all_gather(table, ("group", "dp", "head"), axis=0, tiled=False)
-    table = table.reshape(n_group, n_dp, n_head, rows, EXPERTS)
+    ).reshape(n_col * rows, 2 * EXPERTS)
 
     cached = latent_cache[0]
     scores = (
@@ -74,19 +84,26 @@
 
     res = residual[0].reshape(rows, n_dp, cols).transpose(1, 0, 2).reshape(n_dp, -1, value_width)
     res_rows = res.shape[1]
-    pad = -res_rows % 16
+    facts = jnp.pad(
+        table_high.T[:, None, :], ((0, 0), (0, -res_rows % 16 - 1), (0, value_width - rows))
+    )
     send = jnp.concatenate(
         [
             jnp.broadcast_to(
                 head_rows.reshape(1, heads * reqs, value_width),
                 (n_dp, heads * reqs, value_width),
             ),
-            jnp.pad(res, ((0, 0), (0, pad), (0, 0))),
+            res,
+            facts,
         ],
         axis=1,
     )
+    send, info = lax.optimization_barrier((send, info))
     got = lax.all_to_all(send, "dp", split_axis=0, concat_axis=0, tiled=True)
+    early = lax.optimization_barrier((got, shifts[1], shifts[7], shifts[2], shifts[6]))
+    got, shifts[1], shifts[7], shifts[2], shifts[6] = early
     res_piece = got[:, heads * reqs : heads * reqs + res_rows].reshape(n_dp * rows, cols)
+    mine = got[:, heads * reqs + res_rows, :rows].reshape(1, n_dp * rows) > 0
     values = got[:, : heads * reqs].reshape(n_dp, heads, n_head, rows, value_width)
     partial = jnp.einsum(
         "dhziv,hvc->zdic",
@@ -107,19 +124,25 @@
         concat_axis=0,
         tiled=True,
     )
+    late = lax.optimization_barrier((hidden, shifts[3], shifts[5], shifts[4]))
+    hidden, shifts[3], shifts[5], shifts[4] = late
+    home = lax.dynamic_slice(hidden, (0, dp * rows, 0), (n_dp, rows, cols))
     hidden = hidden.transpose(1, 0, 2).reshape(n_dp * rows, width)
     hidden_f = hidden.astype(f32)
     mean_square = jnp.mean(hidden_f * hidden_f, axis=1, keepdims=True)
     normed = (hidden_f * lax.rsqrt(mean_square + norm_eps) * norm_gain).astype(bf16)
-    home = lax.dynamic_slice(hidden, (dp * rows, 0), (rows, width))
-
-    slot_ids = jnp.arange(CAP, dtype=jnp.int32)
-    mine = lax.dynamic_index_in_dim(lax.dynamic_index_in_dim(table, g, 0, False), z, 1, False)
-    mine = lax.dynamic_index_in_dim(mine, dp, 2, False) > 0
-    before = jnp.cumsum(mine.astype(jnp.int32), axis=1) - mine
-    placed = mine[:, None, :] & (before[:, None, :] == slot_ids[None, :, None])
-    same = jnp.eye(n_dp, dtype=bool)
-    pack = (placed[:, :, None, :] & same[:, None, :, None]).reshape(n_dp * CAP, n_dp * rows)
+
+    def index(shape, axis):
+        return lax.broadcasted_iota(jnp.int32, shape, axis)
+
+    def before(count):
+        a, b = index((count, count), 0), index((count, count), 1)
+        return ((a // rows == b // rows) & (a < b)).astype(bf16)
+
+    count = n_dp * rows
+    slot = jnp.dot(mine.astype(bf16), before(count), preferred_element_type=f32)
+    at, of = index((n_dp * CAP, count), 0), index((n_dp * CAP, count), 1)
+    pack = (at // CAP == of // rows) & mine & (slot == (at % CAP).astype(f32))
     packed = jnp.dot(pack.astype(bf16), normed, preferred_element_type=f32).astype(bf16)
     block = lax.all_gather(packed, ("group", "head"), axis=0, tiled=True)
 
@@ -130,22 +153,35 @@
         active.reshape(n_col, n_dp, CAP, -1).transpose(1, 0, 2, 3).reshape(n_col * n_dp * CAP, -1)
     )
     actives = lax.all_gather(active, ("group", "head"), axis=0, tiled=False)
+    stack = jnp.stack(shifts[::-1] + shifts[::-1])
+    stack = lax.dynamic_slice_in_dim(stack, lax.rem(2 * n_head - 1 - z, n_head), n_head, 0)
+    kept = lax.dynamic_index_in_dim(stack, g, 1, False)
+    given = lax.dynamic_index_in_dim(stack, 1 - g, 1, False)
+    given = lax.ppermute(given, "group", [(0, 1), (1, 0)])
+    down = jnp.where(g == 0, jnp.concatenate([kept, given]), jnp.concatenate([given, kept]))
     out = jnp.einsum("srf,scf->rc", actives, down, preferred_element_type=f32).astype(bf16)
     back = lax.all_to_all(
         out.reshape(n_dp, n_col * CAP, piece), "dp", split_axis=0, concat_axis=0, tiled=True
     )
 
-    ours = lax.dynamic_index_in_dim(table, dp, 1, False).reshape(n_col, rows, EXPERTS)
-    taken = ours > 0
-    ahead = jnp.cumsum(taken.astype(jnp.int32), axis=1) - taken
-    spread = jnp.where(
-        taken[..., None] & (ahead[..., None] == slot_ids), ours[..., None], 0.0
-    )
-    mix = jnp.where(
-        jnp.eye(n_col, dtype=bool)[:, None, None, :, None], spread[:, :, :, None, :], 0.0
-    ).reshape(n_col * rows, EXPERTS * n_col * CAP)
-    mix_high = mix.astype(bf16)
-    mix_low = (mix - mix_high.astype(f32)).astype(bf16)
+    ours_high, ours_low = info[:, :EXPERTS], info[:, EXPERTS:]
+    taken = (ours_high > 0).astype(bf16)
+    count = n_col * rows
+    ahead = jnp.dot(before(count).T, taken, preferred_element_type=f32)
+    ahead = jnp.where(taken > 0, ahead, -1.0).astype(bf16)
+    wide = EXPERTS * n_col * CAP
+    spread = (index((EXPERTS, wide), 0) == index((EXPERTS, wide), 1) // (n_col * CAP)).astype(bf16)
+    at, of = index((count, wide), 0), index((count, wide), 1)
+    hit = (at // rows == of // CAP % n_col) & (
+        jnp.dot(ahead, spread, preferred_element_type=f32) == (of % CAP).astype(f32)
+    )
+    zero = jnp.zeros((), f32)
+    mix_high = jnp.where(
+        hit, jnp.dot(ours_high, spread, preferred_element_type=f32), zero
+    ).astype(bf16)
+    mix_low = jnp.where(
+        hit, jnp.dot(ours_low, spread, preferred_element_type=f32), zero
+    ).astype(bf16)
     back = back.reshape(EXPERTS * n_col * CAP, piece)
     mixed = jnp.dot(mix_high, back, preferred_element_type=f32) + jnp.dot(
         mix_low, back, preferred_element_type=f32
@@ -157,8 +193,8 @@
         concat_axis=0,
         tiled=True,
     )
-    mixture = mixed.transpose(1, 0, 2).reshape(rows, width)
-    layer_out = (home.astype(f32) + mixture.astype(f32)).astype(bf16)
+    layer_out = (home.astype(f32) + mixed.astype(f32)).astype(bf16)
+    layer_out = layer_out.transpose(1, 0, 2).reshape(rows, width)
     return layer_out[None]
 
 

time: 907 us -> 306 us (0.34)
  blocking collectives: 606 us -> 0 us
  starting transfers between devices: 38.5 us -> 54.6 us
  waiting for transfers between devices: 172 us -> 161 us
    all_gather x1 -> x0, blocking collectives: 606 us -> none  [local(): table = lax.all_gather(table, ('group', 'dp', 'head'), axis=0, tiled=False)]
    all_to_all x1, waiting for transfers between devices: 53.9 us -> 0.01 us  [local(): lax.all_to_all(jnp.broadcast_to(info[None], (n_col,) + info.shape), ('gro...]
    ppermute x0 -> x8, waiting for transfers between devices: none -> 31.9 us  [the longest x7 29.3 us: shifted(): lax.ppermute(slab, 'head', [(i, (i + k) % n_head) for i in range(n_head)])]
    all_gather x1, waiting for transfers between devices: 5.56 us -> 24.4 us  [local(): actives = lax.all_gather(active, ('group', 'head'), axis=0, tiled=False)]
    all_to_all x1, waiting for transfers between devices: 16.1 us -> 0.01 us  [local(): got = lax.all_to_all(send, 'dp', split_axis=0, concat_axis=0, tiled=True)]
    ppermute x0 -> x8, starting transfers between devices: none -> 13.3 us  [the longest x7 13 us: shifted(): lax.ppermute(slab, 'head', [(i, (i + k) % n_head) for i in range(n_head)])]
    all_to_all x1, waiting for transfers between devices: 0.01 us -> 13.2 us  [local(): lax.all_to_all(out.reshape(n_dp, n_col * CAP, piece), 'dp', split_axis=0,...]
    unnamed x20 -> x53, local copies, waits for them, and re-layouts: 2.82 us -> 13.9 us
  transfers between devices with their start and end apart: 8 -> 16, of which waited for: 6 -> 12; matrix products, arithmetic and copies ran while one was open for 3% -> 11% of each run, Pallas kernels for 0% -> 0%
where the time goes in v2:
time: 306 us; the launch traced here: 303 us
  waiting for transfers between devices  161 us (53%)
  starting transfers between devices  54.6 us (18%)
  local copies, waits for them, and re-layouts  34.9 us (11%)
  matrix products  32.9 us (11%)
  between operations  13.8 us (5%)
  other arithmetic  5.15 us (2%)
    all_gather x1, waiting for transfers between devices, local(): block = lax.all_gather(packed, ('group', 'head'), axis=0, tiled=True)  69.2 us
    ppermute x7, waiting for transfers between devices, shifted(): lax.ppermute(slab, 'head', [(i, (i + k) % n_head) for i in range(n_head)])  29.3 us
    all_gather x1, waiting for transfers between devices, local(): actives = lax.all_gather(active, ('group', 'head'), axis=0, tiled=False)  24.4 us
    all_to_all x1, waiting for transfers between devices, local(): lax.all_to_all(partial.reshape(n_head, n_dp * rows, cols), 'head', split_...  14.7 us
    unnamed x53, local copies, waits for them, and re-layouts  13.9 us
    all_to_all x1, waiting for transfers between devices, local(): lax.all_to_all(out.reshape(n_dp, n_col * CAP, piece), 'dp', split_axis=0,...  13.2 us
    ppermute x7, starting transfers between devices, shifted(): lax.ppermute(slab, 'head', [(i, (i + k) % n_head) for i in range(n_head)])  13 us
    all_to_all x1, starting transfers between devices, local(): lax.all_to_all(jnp.broadcast_to(info[None], (n_col,) + info.shape), ('gro...  8.57 us
  transfers between devices with their start and end apart: 16, of which 12 were waited for; matrix products, arithmetic and copies ran while one was open for 11% of the time, Pallas kernels for 0%

profile of v2, /device:TPU:8, one launch (start us, length us, event | category | flops | bytes accessed | tf_op | source)
XLA Modules:
  0.0 302.8 jit_solution(5925158735345658109)
XLA Ops:
  6.5 0.9 select_reduce_fusion
  7.5 0.6 broadcast_in_dim.70
  8.2 8.6 %all-to-all-start = ((bf16[16,4,32]{2,1,0:T(4,128)(2,1)}), bf16[16,4,32]{2,1,0:T(4,128)(2,1)S(1)}, u32[]{:S(2)}, u32[]{:S(2)}) async-start(bf16[16,4,32]{2,1,0:T(4,128)(2,1)} %broadcast_in_dim.70), calls=%async_computation | async-start | bytes 32768 | tf_op jit(solution)/shard_map/all_to_all | solution.py:63
  16.8 0.9 reshape_squeeze.7
  18.0 0.7 iota_compare_fusion.2
  18.7 6.1 %fusion.111 = (f32[32,8]{1,0:T(8,128)S(1)}, f32[32,8,192]{2,1,0:T(8,128)S(1)}) fusion(bf16[1,32,8,576]{3,2,1,0:T(8,128)(2,1)} %param.12, pred[32,192]{1,0:T(8,128)(4,1)S(1)} %iota_compare_fusion.2, bf16[1,32,192,576]{3,2,1,0:T(8,128)(2,1)} %param.13), kind=kOutput, calls=%fused_computation.170 | convolution fusion | flops 56819904 | bytes 7576576 | tf_op jit(solution)/shard_map/sub | solution.py:78
  24.8 3.8 %fusion.20 = bf16[32,8,512]{2,1,0:T(8,128)(2,1)S(1)} fusion(bf16[32,192,576]{2,1,0:T(8,128)(2,1)} %bitcast.109, f32[32,8,192]{2,1,0:T(8,128)S(1)} %get-tuple-element.39, f32[32,8]{1,0:T(8,128)S(1)} %get-tuple-element.38), kind=kOutput, calls=%fused_computation.27 | convolution fusion | flops 50561024 | bytes 6751232 | tf_op jit(solution)/shard_map/rhl,rlc->rhc/dot_general | solution.py:80
  29.1 1.1 fusion.36
  30.3 7.4 %all-to-all-start.1 = ((bf16[16,272,128]{2,1,0:T(8,128)(2,1)}), bf16[16,272,128]{2,1,0:T(8,128)(2,1)S(1)}, u32[]{:S(2)}, u32[]{:S(2)}) async-start(bf16[16,272,128]{2,1,0:T(8,128)(2,1)} %fusion.36), calls=%async_computation.1 | async-start | bytes 2228224 | tf_op jit(solution)/shard_map/all_to_all | solution.py:102
  37.7 2.5 dynamic-slice_bitcast_fusion.2
  40.1 1.9 collective-permute-start
  42.1 1.3 collective-permute-start.1
  43.4 1.6 collective-permute-start.2
  45.0 2.5 collective-permute-start.3
  47.5 1.2 copy.66
  48.7 2.0 collective-permute-done
  50.9 5.7 %collective-permute-done.2 = bf16[2,448,128]{2,1,0:T(8,128)(2,1)S(1)} collective-permute-done((bf16[2,448,128]{2,1,0:T(8,128)(2,1)S(1)}, bf16[2,448,128]{2,1,0:T(8,128)(2,1)S(1)}, u32[]{:S(2)}, u32[]{:S(2)}) %collective-permute-start.2) | collective-permute-done | bytes 229408 | tf_op jit(solution)/shard_map/ppermute | solution.py:53
  56.6 0.7 copy-done.7
  57.3 2.4 collective-permute-done.3
  60.2 1.1 copy-done.4
  61.3 0.8 fusion.18
  62.1 1.0 copy.55
  63.0 6.4 %all-to-all-start.2 = ((bf16[8,64,448]{2,1,0:T(8,128)(2,1)}), bf16[8,64,448]{2,1,0:T(8,128)(2,1)S(1)}, u32[]{:S(2)}, u32[]{:S(2)}) async-start(bf16[8,64,448]{2,1,0:T(8,128)(2,1)} %copy.55), calls=%async_computation.2 | async-start | bytes 1048576 | tf_op jit(solution)/shard_map/all_to_all | solution.py:114
  69.4 0.7 slice_convert_fusion
  70.1 1.0 reshape.103
  71.1 14.7 %all-to-all-done.2 = bf16[8,64,448]{2,1,0:T(8,128)(2,1)S(1)} async-done(((bf16[8,64,448]{2,1,0:T(8,128)(2,1)}), bf16[8,64,448]{2,1,0:T(8,128)(2,1)S(1)}, u32[]{:S(2)}, u32[]{:S(2)}) %all-to-all-start.2) | async-done | bytes 458784 | tf_op jit(solution)/shard_map/all_to_all | solution.py:114
  85.8 1.1 broadcast_in_dim.71
  86.9 7.2 %all-to-all-start.3 = ((bf16[16,64,448]{2,1,0:T(8,128)(2,1)}), bf16[16,64,448]{2,1,0:T(8,128)(2,1)S(1)}, u32[]{:S(2)}, u32[]{:S(2)}) async-start(bf16[16,64,448]{2,1,0:T(8,128)(2,1)} %broadcast_in_dim.71), calls=%async_computation.3 | async-start | bytes 2097152 | tf_op jit(solution)/shard_map/all_to_all | solution.py:120
  94.3 5.0 %collective-permute-start.5 = (bf16[2,448,128]{2,1,0:T(8,128)(2,1)}, bf16[2,448,128]{2,1,0:T(8,128)(2,1)S(1)}, u32[]{:S(2)}, u32[]{:S(2)}) collective-permute-start(bf16[2,448,128]{2,1,0:T(8,128)(2,1)} %get-tuple-element.32), channel_id=1, source_target_pairs={{0,5},{1,6},{2,7},{3,0},{4,1},{5,2},{6,3},{7,4},{8,13},{9,14},{10,... | collective-permute-start | bytes 688136 | tf_op jit(solution)/shard_map/ppermute | solution.py:53
  99.3 0.6 collective-permute-start.6
  99.9 0.8 compare_reduce_fusion
  101.1 17.7 %collective-permute-done.4 = bf16[2,448,128]{2,1,0:T(8,128)(2,1)S(1)} collective-permute-done((bf16[2,448,128]{2,1,0:T(8,128)(2,1)}, bf16[2,448,128]{2,1,0:T(8,128)(2,1)S(1)}, u32[]{:S(2)}, u32[]{:S(2)}) %collective-permute-start.4) | collective-permute-done | bytes 229408 | tf_op jit(solution)/shard_map/ppermute | solution.py:53
  118.9 1.3 collective-permute-done.5
  120.8 2.6 copy.57
  123.4 3.1 %reshape.104 = f32[64,7168]{1,0:T(8,128)} reshape(f32[64,16,448]{2,1,0:T(8,128)} %copy.57) | data formatting | bytes 3670016 | tf_op jit(solution)/shard_map/convert_element_type | solution.py:131
  126.4 2.8 convolution_convert_fusion
  129.3 69.2 %all-gather.3.cloned.1.call-done = bf16[768,7168]{1,0:T(8,128)(2,1)} async-done(((bf16[48,7168]{1,0:T(8,128)(2,1)}), bf16[768,7168]{1,0:T(8,128)(2,1)}) %all-gather.3.cloned.1.call-update) | async-done | bytes 11010064 | tf_op jit(solution)/shard_map/all_gather | solution.py:147
  198.5 6.9 %fusion.13 = f32[768,128]{1,0:T(8,128)S(1)} fusion(bf16[768,7168]{1,0:T(8,128)(2,1)} %all-gather.3.cloned.1.call-done, bf16[1,7168,128]{2,1,0:T(8,128)(2,1)S(1)} %copy-done), kind=kOutput, calls=%fused_computation.18 | convolution fusion | flops 1409286144 | bytes 13238272 | tf_op jit(solution)/shard_map/dot_general | solution.py:149
  206.4 3.0 fusion.28
  209.6 0.8 all_gather_reshape.3
  210.5 1.0 bitcast_dynamic-update-slice_fusion.14
  211.5 1.0 bitcast_dynamic-update-slice_fusion.12
  212.5 1.0 bitcast_dynamic-update-slice_fusion.10
  213.5 1.0 bitcast_dynamic-update-slice_fusion.8
  214.5 1.0 bitcast_dynamic-update-slice_fusion.6
  215.4 1.0 bitcast_dynamic-update-slice_fusion.4
  216.4 1.0 bitcast_dynamic-update-slice_fusion.2
  217.4 1.0 bitcast_dynamic-update-slice_fusion
  218.4 1.0 bitcast_dynamic-update-slice_fusion.13
  219.4 1.0 bitcast_dynamic-update-slice_fusion.9
  220.6 1.0 bitcast_dynamic-update-slice_fusion.1
  221.5 1.4 dynamic-slice_bitcast_fusion.1
  223.2 2.5 collective-permute-done.7
  225.7 24.4 %all-gather.5.cloned.1.call-done = bf16[16,768,128]{2,1,0:T(8,128)(2,1)} async-done(((bf16[1,768,128]{2,1,0:T(8,128)(2,1)}), bf16[16,768,128]{2,1,0:T(8,128)(2,1)}) %all-gather.5.cloned.1.call-update) | async-done | bytes 3145744 | tf_op jit(solution)/shard_map/all_gather | solution.py:155
  250.1 5.5 %fusion.17 = bf16[768,448]{0,1:T(8,128)(2,1)} fusion(bf16[16,768,128]{2,1,0:T(8,128)(2,1)} %all-gather.5.cloned.1.call-done, bf16[8,448,128]{2,1,0:T(8,128)(2,1)} %collective-permute-done.7, bf16[8,448,128]{2,1,0:T(8,128)(2,1)} %get-tuple-element.29, pred[]{:T(512)S(6)} %eq.64), kind=kOutput, calls=%fused_computation.24 | convolution fusion | flops 1412382720 | bytes 5668865 | tf_op jit(solution)/shard_map/srf,scf->rc/dot_general | solution.py:162
  255.6 2.3 copy.59
  257.9 7.3 %all-to-all-start.4 = ((bf16[16,48,448]{2,1,0:T(8,128)(2,1)}), bf16[16,48,448]{2,1,0:T(8,128)(2,1)}, u32[]{:S(2)}, u32[]{:S(2)}) async-start(bf16[16,48,448]{2,1,0:T(8,128)(2,1)} %bitcast.110), calls=%async_computation.4 | async-start | bytes 1572864 | tf_op jit(solution)/shard_map/all_to_all | solution.py:163
  265.7 13.2 %all-to-all-done.4 = bf16[16,48,448]{2,1,0:T(8,128)(2,1)} async-done(((bf16[16,48,448]{2,1,0:T(8,128)(2,1)}), bf16[16,48,448]{2,1,0:T(8,128)(2,1)}, u32[]{:S(2)}, u32[]{:S(2)}) %all-to-all-start.4) | async-done | bytes 688160 | tf_op jit(solution)/shard_map/all_to_all | solution.py:163
  278.9 1.5 fusion.34
  280.4 1.6 fusion.33
  282.0 0.7 reshape.102
  282.7 4.5 %all-to-all-start.5 = ((bf16[16,4,448]{2,1,0:T(4,128)(2,1)}), bf16[16,4,448]{2,1,0:T(4,128)(2,1)S(1)}, u32[]{:S(2)}, u32[]{:S(2)}) async-start(bf16[16,4,448]{2,1,0:T(4,128)(2,1)} %reshape.102), calls=%async_computation.5 | async-start | bytes 131072 | tf_op jit(solution)/shard_map/all_to_all | solution.py:189
  287.1 8.0 %all-to-all-done.5 = bf16[16,4,448]{2,1,0:T(4,128)(2,1)S(1)} async-done(((bf16[16,4,448]{2,1,0:T(4,128)(2,1)}), bf16[16,4,448]{2,1,0:T(4,128)(2,1)S(1)}, u32[]{:S(2)}, u32[]{:S(2)}) %all-to-all-start.5) | async-done | bytes 57376 | tf_op jit(solution)/shard_map/all_to_all | solution.py:189
  295.2 0.8 broadcast_in_dim_reshape.3
  (83 shorter events, 5.1 us)
Async XLA Ops:
  6.5 192.0 %copy-start = (bf16[1,7168,128]{2,1,0:T(8,128)(2,1)S(1)}, bf16[1,7168,128]{2,1,0:T(8,128)(2,1)}, u32[]{:S(2)}) copy-start(bf16[1,7168,128]{2,1,0:T(8,128)(2,1)} %param.21) | copy-start | bytes 5505028
  8.2 22.1 %all-to-all-start = ((bf16[16,4,32]{2,1,0:T(4,128)(2,1)}), bf16[16,4,32]{2,1,0:T(4,128)(2,1)S(1)}, u32[]{:S(2)}, u32[]{:S(2)}) async-start(bf16[16,4,32]{2,1,0:T(4,128)(2,1)} %broadcast_in_dim.70), calls=%async_computation | async-start | bytes 32768 | tf_op jit(solution)/shard_map/all_to_all | solution.py:63
  24.8 3.8 %copy-start.2 = (bf16[8,512,128]{2,1,0:T(8,128)(2,1)S(1)}, bf16[8,512,128]{2,1,0:T(8,128)(2,1)}, u32[]{:S(2)}) copy-start(bf16[8,512,128]{2,1,0:T(8,128)(2,1)} %param.15) | copy-start | bytes 3145732
  30.3 29.5 %all-to-all-start.1 = ((bf16[16,272,128]{2,1,0:T(8,128)(2,1)}), bf16[16,272,128]{2,1,0:T(8,128)(2,1)S(1)}, u32[]{:S(2)}, u32[]{:S(2)}) async-start(bf16[16,272,128]{2,1,0:T(8,128)(2,1)} %fusion.36), calls=%async_computation.1 | async-start | bytes 2228224 | tf_op jit(solution)/shard_map/all_to_all | solution.py:102
  37.7 9.9 %copy-start.3 = (bf16[1024,448]{0,1:T(8,128)(2,1)S(1)}, bf16[1024,448]{0,1:T(8,128)(2,1)}, u32[]{:S(2)}) copy-start(bf16[1024,448]{0,1:T(8,128)(2,1)} %param.16) | copy-start | bytes 2752516
  40.1 10.6 %collective-permute-start = (bf16[2,448,128]{2,1,0:T(8,128)(2,1)S(1)}, bf16[2,448,128]{2,1,0:T(8,128)(2,1)S(1)}, u32[]{:S(2)}, u32[]{:S(2)}) collective-permute-start(bf16[2,448,128]{2,1,0:T(8,128)(2,1)S(1)} %get-tuple-element.37), channel_id=1, source_target_pairs={{0,1},{1,2},{2,3},{3,4},{4,5},{5,6},{6,7},{7,0},{8,9},{9,10},{10,1... | collective-permute-start | bytes 688136 | tf_op jit(solution)/shard_map/ppermute | solution.py:53
  42.1 8.9 %collective-permute-start.1 = (bf16[2,448,128]{2,1,0:T(8,128)(2,1)S(1)}, bf16[2,448,128]{2,1,0:T(8,128)(2,1)S(1)}, u32[]{:S(2)}, u32[]{:S(2)}) collective-permute-start(bf16[2,448,128]{2,1,0:T(8,128)(2,1)S(1)} %get-tuple-element.36), channel_id=1, source_target_pairs={{0,7},{1,0},{2,1},{3,2},{4,3},{5,4},{6,5},{7,6},{8,15},{9,8},{10,9... | collective-permute-start | bytes 688136 | tf_op jit(solution)/shard_map/ppermute | solution.py:53
  43.4 13.3 %collective-permute-start.2 = (bf16[2,448,128]{2,1,0:T(8,128)(2,1)S(1)}, bf16[2,448,128]{2,1,0:T(8,128)(2,1)S(1)}, u32[]{:S(2)}, u32[]{:S(2)}) collective-permute-start(bf16[2,448,128]{2,1,0:T(8,128)(2,1)S(1)} %get-tuple-element.35), channel_id=1, source_target_pairs={{0,2},{1,3},{2,4},{3,5},{4,6},{5,7},{6,0},{7,1},{8,10},{9,11},{10,... | collective-permute-start | bytes 688136 | tf_op jit(solution)/shard_map/ppermute | solution.py:53
  45.0 14.7 %collective-permute-start.3 = (bf16[2,448,128]{2,1,0:T(8,128)(2,1)S(1)}, bf16[2,448,128]{2,1,0:T(8,128)(2,1)}, u32[]{:S(2)}, u32[]{:S(2)}) collective-permute-start(bf16[2,448,128]{2,1,0:T(8,128)(2,1)S(1)} %get-tuple-element.34), channel_id=1, source_target_pairs={{0,6},{1,7},{2,0},{3,1},{4,2},{5,3},{6,4},{7,5},{8,14},{9,15},{10,... | collective-permute-start | bytes 688136 | tf_op jit(solution)/shard_map/ppermute | solution.py:53
  50.7 5.9 %copy-start.5 = (bf16[2,448,128]{2,1,0:T(8,128)(2,1)}, bf16[2,448,128]{2,1,0:T(8,128)(2,1)S(1)}, u32[]{:S(2)}) copy-start(bf16[2,448,128]{2,1,0:T(8,128)(2,1)S(1)} %collective-permute-done) | copy-start | bytes 688132
  50.9 5.7 %copy-start.9 = (bf16[2,448,128]{2,1,0:T(8,128)(2,1)}, bf16[2,448,128]{2,1,0:T(8,128)(2,1)S(1)}, u32[]{:S(2)}) copy-start(bf16[2,448,128]{2,1,0:T(8,128)(2,1)S(1)} %collective-permute-done.1) | copy-start | bytes 688132
  56.6 0.7 copy-start.7
  59.7 9.7 %copy-start.1 = (bf16[16,272,128]{2,1,0:T(8,128)(2,1)}, bf16[16,272,128]{2,1,0:T(8,128)(2,1)S(1)}, u32[]{:S(2)}) copy-start(bf16[16,272,128]{2,1,0:T(8,128)(2,1)S(1)} %all-to-all-done.1) | copy-start | bytes 3342340
  59.7 1.6 copy-start.4
  63.0 22.7 %all-to-all-start.2 = ((bf16[8,64,448]{2,1,0:T(8,128)(2,1)}), bf16[8,64,448]{2,1,0:T(8,128)(2,1)S(1)}, u32[]{:S(2)}, u32[]{:S(2)}) async-start(bf16[8,64,448]{2,1,0:T(8,128)(2,1)} %copy.55), calls=%async_computation.2 | async-start | bytes 1048576 | tf_op jit(solution)/shard_map/all_to_all | solution.py:114
  86.9 33.2 %all-to-all-start.3 = ((bf16[16,64,448]{2,1,0:T(8,128)(2,1)}), bf16[16,64,448]{2,1,0:T(8,128)(2,1)S(1)}, u32[]{:S(2)}, u32[]{:S(2)}) async-start(bf16[16,64,448]{2,1,0:T(8,128)(2,1)} %broadcast_in_dim.71), calls=%async_computation.3 | async-start | bytes 2097152 | tf_op jit(solution)/shard_map/all_to_all | solution.py:120
  94.2 104.4 %all-gather.3.cloned.1.call-start = ((), (), s32[]{:S(2)}) async-start(), calls=%async_computation.6 | async-start | bytes 11698176 | tf_op jit(solution)/shard_map/all_gather | solution.py:147
  94.2 24.7 %collective-permute-start.4 = (bf16[2,448,128]{2,1,0:T(8,128)(2,1)}, bf16[2,448,128]{2,1,0:T(8,128)(2,1)S(1)}, u32[]{:S(2)}, u32[]{:S(2)}) collective-permute-start(bf16[2,448,128]{2,1,0:T(8,128)(2,1)} %get-tuple-element.33), channel_id=1, source_target_pairs={{0,3},{1,4},{2,5},{3,6},{4,7},{5,0},{6,1},{7,2},{8,11},{9,12},{10,... | collective-permute-start | bytes 688136 | tf_op jit(solution)/shard_map/ppermute | solution.py:53
  94.3 25.8 %collective-permute-start.5 = (bf16[2,448,128]{2,1,0:T(8,128)(2,1)}, bf16[2,448,128]{2,1,0:T(8,128)(2,1)S(1)}, u32[]{:S(2)}, u32[]{:S(2)}) collective-permute-start(bf16[2,448,128]{2,1,0:T(8,128)(2,1)} %get-tuple-element.32), channel_id=1, source_target_pairs={{0,5},{1,6},{2,7},{3,0},{4,1},{5,2},{6,3},{7,4},{8,13},{9,14},{10,... | collective-permute-start | bytes 688136 | tf_op jit(solution)/shard_map/ppermute | solution.py:53
  99.3 20.8 %collective-permute-start.6 = (bf16[2,448,128]{2,1,0:T(8,128)(2,1)}, bf16[2,448,128]{2,1,0:T(8,128)(2,1)}, u32[]{:S(2)}, u32[]{:S(2)}) collective-permute-start(bf16[2,448,128]{2,1,0:T(8,128)(2,1)} %get-tuple-element.31), channel_id=1, source_target_pairs={{0,4},{1,5},{2,6},{3,7},{4,0},{5,1},{6,2},{7,3},{8,12},{9,13},{10,... | collective-permute-start | bytes 688136 | tf_op jit(solution)/shard_map/ppermute | solution.py:53
  118.9 4.5 %copy-start.11 = (bf16[2,448,128]{2,1,0:T(8,128)(2,1)}, bf16[2,448,128]{2,1,0:T(8,128)(2,1)S(1)}, u32[]{:S(2)}) copy-start(bf16[2,448,128]{2,1,0:T(8,128)(2,1)S(1)} %collective-permute-done.4) | copy-start | bytes 688132
  120.1 3.2 %copy-start.13 = (bf16[2,448,128]{2,1,0:T(8,128)(2,1)}, bf16[2,448,128]{2,1,0:T(8,128)(2,1)S(1)}, u32[]{:S(2)}) copy-start(bf16[2,448,128]{2,1,0:T(8,128)(2,1)S(1)} %collective-permute-done.5) | copy-start | bytes 688132
  120.8 5.7 %copy-start.15 = (f32[7168]{0:T(1024)S(1)}, f32[7168]{0:T(1024)}, u32[]{:S(2)}) copy-start(f32[7168]{0:T(1024)} %param.18) | copy-start | bytes 86020
  129.3 120.9 %all-gather.5.cloned.1.call-start = ((), (), s32[]{:S(2)}) async-start(), calls=%async_computation.7 | async-start | bytes 3342336 | tf_op jit(solution)/shard_map/all_gather | solution.py:155
  198.5 7.3 %copy-start.16 = (bf16[768,7168]{1,0:T(8,128)(2,1)S(1)}, bf16[768,7168]{1,0:T(8,128)(2,1)}, u32[]{:S(2)}) copy-start(bf16[768,7168]{1,0:T(8,128)(2,1)} %all-gather.3.cloned.1.call-done) | copy-start | bytes 33030148
  198.5 7.8 %copy-start.17 = (bf16[1,7168,128]{2,1,0:T(8,128)(2,1)S(1)}, bf16[1,7168,128]{2,1,0:T(8,128)(2,1)}, u32[]{:S(2)}) copy-start(bf16[1,7168,128]{2,1,0:T(8,128)(2,1)} %param.22) | copy-start | bytes 5505028
  209.6 10.9 %copy-start.6 = (bf16[2,448,128]{2,1,0:T(8,128)(2,1)S(1)}, bf16[2,448,128]{2,1,0:T(8,128)(2,1)}, u32[]{:S(2)}) copy-start(bf16[2,448,128]{2,1,0:T(8,128)(2,1)} %copy-done.5) | copy-start | bytes 688132
  210.4 10.0 %copy-start.8 = (bf16[2,448,128]{2,1,0:T(8,128)(2,1)S(1)}, bf16[2,448,128]{2,1,0:T(8,128)(2,1)}, u32[]{:S(2)}) copy-start(bf16[2,448,128]{2,1,0:T(8,128)(2,1)} %copy-done.7) | copy-start | bytes 688132
  210.5 7.9 %copy-start.10 = (bf16[2,448,128]{2,1,0:T(8,128)(2,1)S(1)}, bf16[2,448,128]{2,1,0:T(8,128)(2,1)}, u32[]{:S(2)}) copy-start(bf16[2,448,128]{2,1,0:T(8,128)(2,1)} %copy-done.9) | copy-start | bytes 688132
  210.5 8.9 %copy-start.14 = (bf16[2,448,128]{2,1,0:T(8,128)(2,1)S(1)}, bf16[2,448,128]{2,1,0:T(8,128)(2,1)}, u32[]{:S(2)}) copy-start(bf16[2,448,128]{2,1,0:T(8,128)(2,1)} %copy-done.13) | copy-start | bytes 688132
  210.5 9.9 %copy-start.12 = (bf16[2,448,128]{2,1,0:T(8,128)(2,1)S(1)}, bf16[2,448,128]{2,1,0:T(8,128)(2,1)}, u32[]{:S(2)}) copy-start(bf16[2,448,128]{2,1,0:T(8,128)(2,1)} %copy-done.11) | copy-start | bytes 688132
  222.9 2.8 collective-permute-start.7
  257.9 21.0 %all-to-all-start.4 = ((bf16[16,48,448]{2,1,0:T(8,128)(2,1)}), bf16[16,48,448]{2,1,0:T(8,128)(2,1)}, u32[]{:S(2)}, u32[]{:S(2)}) async-start(bf16[16,48,448]{2,1,0:T(8,128)(2,1)} %bitcast.110), calls=%async_computation.4 | async-start | bytes 1572864 | tf_op jit(solution)/shard_map/all_to_all | solution.py:163
  282.7 12.4 %all-to-all-start.5 = ((bf16[16,4,448]{2,1,0:T(4,128)(2,1)}), bf16[16,4,448]{2,1,0:T(4,128)(2,1)S(1)}, u32[]{:S(2)}, u32[]{:S(2)}) async-start(bf16[16,4,448]{2,1,0:T(4,128)(2,1)} %reshape.102), calls=%async_computation.5 | async-start | bytes 131072 | tf_op jit(solution)/shard_map/all_to_all | solution.py:189
Sparse Core Ops, SparseCore 0:
  129.4 69.1 all-gather.2
  210.6 39.5 all-gather.4
